TPU v7x, 256 devices: a whole 4x4x8 slice. The times are simulated.
256 devices in a mesh: section: 32 (over y_hi, z, core), ctx: 8 (over y_lo, x).
Axes of the slice: x: 4, y: 4 (y_hi: 2, y_lo: 2; y = y_hi * 2 + y_lo), z: 8, core: 2. Of those that a mesh axis runs over, the one named last changes fastest.
Arguments:
- queries: bfloat16 [32, 1024, 8192], P('section', 'ctx'), may hold values from -6 to 6
- key_states: bfloat16 [32, 1024, 1024], P('section', 'ctx'), may hold values from -6 to 6
- value_states: bfloat16 [32, 1024, 1024], P('section', 'ctx'), may hold values from -1.5 to 1.5
- out_grad: bfloat16 [32, 1024, 8192], P('section', 'ctx'), may hold values from -6 to 6
- node_end: int32 [32, 1024], P('section'), may hold values from 1 to 1024, as said below
- block_list: int32 [32, 8, 8], P('section'), may hold values from 0 to 7, as said below
- block_count: int32 [32, 8], P('section'), may hold values from 1 to 8, as said below
Outputs:
- query_grads: bfloat16 [32, 1024, 8192], P('section', 'ctx')
- key_grads: bfloat16 [32, 1024, 1024], P('section', 'ctx')
- value_grads: bfloat16 [32, 1024, 1024], P('section', 'ctx')
Inputs may be any that keep to these rules, and one draw needn't show every extreme that they name: Each section packs search trees one after another, each in preorder; node_end[s, j] is one past the last node of node j's subtree, so j is an ancestor of i (or i itself) exactly when j <= i < node_end[s, j]. Row b of block_list[s] lists, in increasing order, every key block that holds an ancestor (or the node itself) of some node of query block b, and no other; b itself is always listed; entries after the first block_count[s, b] are 0. block_count[s, b] is the number of listed key blocks of query block b, at most b + 1.
All inputs are finite; a program needn't handle non-finite values.
Results may differ from a plain program's by a relative error of at most 0.0053.
Values may be sent and summed in bfloat16 or wider, within the bound.
No kernel may reach another device: no remote copies, remote signals or barrier semaphores. Data moves between devices by JAX's collectives and lax.ppermute only.
A program may use at most 128 MiB of HBM per device.

v0:
```python
import math
import jax
import jax.numpy as jnp
from jax import lax
from jax.sharding import PartitionSpec as P

HEADS = 64
KV_HEADS = 8
HEAD_DIM = 128
BLK = 128


def from_behind(block, axis, distance):
    devices = range(lax.axis_size(axis))
    route = [((i - distance) % len(devices), i) for i in devices]
    return lax.ppermute(block, axis, route)


def allowed_mask(end_row, list_rows, count_row):
    length = end_row.shape[0]
    block_total = list_rows.shape[0]
    position = jnp.arange(length, dtype=jnp.int32)
    ancestry = (position[None, :] <= position[:, None]) & (position[:, None] < end_row[None, :])
    entries = jnp.arange(block_total, dtype=jnp.int32)
    listed = jnp.any(
        (list_rows[:, :, None] == entries[None, None, :])
        & (entries[None, :, None] < count_row[:, None, None]),
        axis=1,
    )
    spread = jnp.repeat(jnp.repeat(listed, BLK, axis=0), BLK, axis=1)
    return ancestry & spread


def head_block(query_rows, grad_rows, key_rows, value_rows, allowed):
    row_total = query_rows.shape[0]
    scale = 1.0 / math.sqrt(HEAD_DIM)
    query_heads = query_rows.reshape(row_total, -1, HEAD_DIM)
    grad_heads = grad_rows.reshape(row_total, -1, HEAD_DIM)
    scores = (
        jnp.einsum("qhd,kd->hqk", query_heads, key_rows, preferred_element_type=jnp.float32) * scale
    )
    scores = jnp.where(allowed[None], scores, -jnp.inf)
    row_max = jnp.max(scores, axis=2, keepdims=True)
    exponent = jnp.exp(scores - row_max)
    attention = exponent / jnp.sum(exponent, axis=2, keepdims=True)
    attention_half = attention.astype(jnp.bfloat16)
    weight_grad = jnp.einsum(
        "qhd,kd->hqk", grad_heads, value_rows, preferred_element_type=jnp.float32
    )
    row_delta = jnp.sum(attention * weight_grad, axis=2, keepdims=True)
    score_grad = (attention * (weight_grad - row_delta) * scale).astype(jnp.bfloat16)
    query_grad = jnp.einsum(
        "hqk,kd->qhd", score_grad, key_rows, preferred_element_type=jnp.float32
    ).reshape(row_total, -1)
    key_grad = jnp.einsum(
        "hqk,qhd->kd", score_grad, query_heads, preferred_element_type=jnp.float32
    )
    value_grad = jnp.einsum(
        "hqk,qhd->kd", attention_half, grad_heads, preferred_element_type=jnp.float32
    )
    return (query_grad, key_grad, value_grad)


def per_device(queries, key_states, value_states, out_grad, node_end, block_list, block_count):
    node_count = queries.shape[1]
    allowed = allowed_mask(node_end[0], block_list[0], block_count[0])
    ratio = HEADS // KV_HEADS
    full_keys, full_values = (
        lax.all_gather(key_states, "ctx", axis=1, tiled=True),
        lax.all_gather(value_states, "ctx", axis=1, tiled=True),
    )
    length = full_keys.shape[1]
    row_allowed = lax.dynamic_slice_in_dim(
        allowed, lax.axis_index("ctx") * node_count, node_count, 0
    )
    width = ratio * HEAD_DIM

    def per_group(group_index, carry):
        query_acc, pair_acc = carry
        query_grad, key_grad, value_grad = head_block(
            lax.dynamic_slice_in_dim(queries[0], group_index * width, width, 1),
            lax.dynamic_slice_in_dim(out_grad[0], group_index * width, width, 1),
            lax.dynamic_slice_in_dim(full_keys[0], group_index * HEAD_DIM, HEAD_DIM, 1),
            lax.dynamic_slice_in_dim(full_values[0], group_index * HEAD_DIM, HEAD_DIM, 1),
            row_allowed,
        )
        query_acc = lax.dynamic_update_slice_in_dim(
            query_acc, query_grad.astype(jnp.bfloat16), group_index * width, 1
        )
        pair_acc = lax.dynamic_update_slice_in_dim(
            pair_acc, jnp.stack([key_grad, value_grad]), group_index * HEAD_DIM, 2
        )
        return (query_acc, pair_acc)

    start_query = jnp.zeros((node_count, queries.shape[2]), jnp.bfloat16)
    start_pair = jnp.zeros((2, length, key_states.shape[2]), jnp.float32)
    query_acc, pair_acc = lax.fori_loop(0, KV_HEADS, per_group, (start_query, start_pair))
    summed = lax.psum_scatter(pair_acc, "ctx", scatter_dimension=1, tiled=True)
    query_nodes = query_acc[None]
    pair_nodes = summed.astype(jnp.bfloat16)
    query_sent = from_behind(query_nodes, "section", -1)
    pair_sent = from_behind(pair_nodes, "section", -1)
    return (query_sent, pair_sent[0:1], pair_sent[1:2])


def solution(mesh):
    placed = (
        P("section", "ctx", None),
        P("section", "ctx", None),
        P("section", "ctx", None),
        P("section", "ctx", None),
        P("section", None),
        P("section", None, None),
        P("section", None),
    )
    return jax.shard_map(
        per_device,
        mesh=mesh,
        in_specs=placed,
        out_specs=(P("section", "ctx", None), P("section", "ctx", None), P("section", "ctx", None)),
        check_vma=False,
    )
```

profile of v0, /device:TPU:6, one launch (start us, length us, event | category | flops | bytes accessed | tf_op | source)
XLA Modules:
  0.0 464.5 jit_solution(3999073993154204466)
XLA Ops:
  11.5 42.9 %all-gather.3.cloned.1.call-done = bf16[1,1024,1024]{2,1,0:T(8,128)(2,1)} async-done(((bf16[1,128,1024]{2,1,0:T(8,128)(2,1)}), bf16[1,1024,1024]{2,1,0:T(8,128)(2,1)}) %all-gather.3.cloned.1.call-update) | async-done | bytes 2097168 | tf_op jit(solution)/shard_map/all_gather | solution.py:69
  54.4 45.2 %all-gather.5.cloned.1.call-done = bf16[1,1024,1024]{2,1,0:T(8,128)(2,1)} async-done(((bf16[1,128,1024]{2,1,0:T(8,128)(2,1)}), bf16[1,1024,1024]{2,1,0:T(8,128)(2,1)}) %all-gather.5.cloned.1.call-update) | async-done | bytes 2097168 | tf_op jit(solution)/shard_map/all_gather | solution.py:70
  101.1 4.3 broadcast_in_dim.57
  105.4 228.4 %while.15 = (s32[]{:T(128)}, bf16[128,8192]{1,0:T(8,128)(2,1)}, f32[2,1024,1024]{2,1,0:T(8,128)}, bf16[1,1024,1024]{2,1,0:T(8,128)(2,1)}, pred[128,1024]{0,1:T(8...) while((s32[]{:T(128)}, bf16[128,8192]{1,0:T(8,128)(2,1)}, ...), condition=%wide.region_5.6_spmd, body=%wide.region_1.5_spmd.sunk | while | flops 1363547136 | bytes 46289144 | solution.py:97
  110.4 4.3 fusion.88
  114.7 7.1 %fusion.91 = f32[1,1024,128]{2,1,0:T(8,128)S(1)} fusion(bf16[128,8,128]{0,2,1:T(8,128)(2,1)S(1)} %bitcast.121, f32[1024,128,8]{1,0,2:T(8,128)} %fusion.87, f32[8,128,1024]{1,2,0:T(8,128)} %get-tuple-element.238, f32[8,128]{1,0:T(8,128)S(1)} %get-tuple-element.239), kind=kOutput, calls=%fused_computation.19.clone.1 | convolution fusion | flops 275777536 | bytes 9179136 | tf_op jit(solution)/shard_map/while/body/eval_jaxpr/hqk,qhd->kd/dot_general | solution.py:55
  121.7 7.3 %fusion.89 = bf16[128,8,128]{2,0,1:T(8,128)(2,1)S(1)} fusion(f32[1024,128,8]{1,0,2:T(8,128)} %fusion.87, bf16[1,1024,1024]{2,1,0:T(8,128)(2,1)} %get-tuple-element.269, s32[]{:T(128)S(6)} %select_n.45, f32[8,128,1024]{1,2,0:T(8,128)} %get-tuple-element.238, f32[8,128]{1,0:T(8,128)S(1)} %get-tuple-element.239), kind=kOutput, calls=%fused_computation.21.clone.1 | convolution fusion | flops 275908608 | bytes 17309700 | tf_op jit(solution)/shard_map/while/body/eval_jaxpr/hqk,kd->qhd/dot_general | solution.py:52
  139.0 4.3 fusion.88
  143.2 7.1 %fusion.91 = f32[1,1024,128]{2,1,0:T(8,128)S(1)} fusion(bf16[128,8,128]{0,2,1:T(8,128)(2,1)S(1)} %bitcast.121, f32[1024,128,8]{1,0,2:T(8,128)} %fusion.87, f32[8,128,1024]{1,2,0:T(8,128)} %get-tuple-element.238, f32[8,128]{1,0:T(8,128)S(1)} %get-tuple-element.239), kind=kOutput, calls=%fused_computation.19.clone.1 | convolution fusion | flops 275777536 | bytes 9179136 | tf_op jit(solution)/shard_map/while/body/eval_jaxpr/hqk,qhd->kd/dot_general | solution.py:55
  150.3 7.3 %fusion.89 = bf16[128,8,128]{2,0,1:T(8,128)(2,1)S(1)} fusion(f32[1024,128,8]{1,0,2:T(8,128)} %fusion.87, bf16[1,1024,1024]{2,1,0:T(8,128)(2,1)} %get-tuple-element.269, s32[]{:T(128)S(6)} %select_n.45, f32[8,128,1024]{1,2,0:T(8,128)} %get-tuple-element.238, f32[8,128]{1,0:T(8,128)S(1)} %get-tuple-element.239), kind=kOutput, calls=%fused_computation.21.clone.1 | convolution fusion | flops 275908608 | bytes 17309700 | tf_op jit(solution)/shard_map/while/body/eval_jaxpr/hqk,kd->qhd/dot_general | solution.py:52
  167.5 4.2 fusion.88
  171.8 7.1 %fusion.91 = f32[1,1024,128]{2,1,0:T(8,128)S(1)} fusion(bf16[128,8,128]{0,2,1:T(8,128)(2,1)S(1)} %bitcast.121, f32[1024,128,8]{1,0,2:T(8,128)} %fusion.87, f32[8,128,1024]{1,2,0:T(8,128)} %get-tuple-element.238, f32[8,128]{1,0:T(8,128)S(1)} %get-tuple-element.239), kind=kOutput, calls=%fused_computation.19.clone.1 | convolution fusion | flops 275777536 | bytes 9179136 | tf_op jit(solution)/shard_map/while/body/eval_jaxpr/hqk,qhd->kd/dot_general | solution.py:55
  178.9 7.3 %fusion.89 = bf16[128,8,128]{2,0,1:T(8,128)(2,1)S(1)} fusion(f32[1024,128,8]{1,0,2:T(8,128)} %fusion.87, bf16[1,1024,1024]{2,1,0:T(8,128)(2,1)} %get-tuple-element.269, s32[]{:T(128)S(6)} %select_n.45, f32[8,128,1024]{1,2,0:T(8,128)} %get-tuple-element.238, f32[8,128]{1,0:T(8,128)S(1)} %get-tuple-element.239), kind=kOutput, calls=%fused_computation.21.clone.1 | convolution fusion | flops 275908608 | bytes 17309700 | tf_op jit(solution)/shard_map/while/body/eval_jaxpr/hqk,kd->qhd/dot_general | solution.py:52
  196.1 4.3 fusion.88
  200.3 7.1 %fusion.91 = f32[1,1024,128]{2,1,0:T(8,128)S(1)} fusion(bf16[128,8,128]{0,2,1:T(8,128)(2,1)S(1)} %bitcast.121, f32[1024,128,8]{1,0,2:T(8,128)} %fusion.87, f32[8,128,1024]{1,2,0:T(8,128)} %get-tuple-element.238, f32[8,128]{1,0:T(8,128)S(1)} %get-tuple-element.239), kind=kOutput, calls=%fused_computation.19.clone.1 | convolution fusion | flops 275777536 | bytes 9179136 | tf_op jit(solution)/shard_map/while/body/eval_jaxpr/hqk,qhd->kd/dot_general | solution.py:55
  207.4 7.3 %fusion.89 = bf16[128,8,128]{2,0,1:T(8,128)(2,1)S(1)} fusion(f32[1024,128,8]{1,0,2:T(8,128)} %fusion.87, bf16[1,1024,1024]{2,1,0:T(8,128)(2,1)} %get-tuple-element.269, s32[]{:T(128)S(6)} %select_n.45, f32[8,128,1024]{1,2,0:T(8,128)} %get-tuple-element.238, f32[8,128]{1,0:T(8,128)S(1)} %get-tuple-element.239), kind=kOutput, calls=%fused_computation.21.clone.1 | convolution fusion | flops 275908608 | bytes 17309700 | tf_op jit(solution)/shard_map/while/body/eval_jaxpr/hqk,kd->qhd/dot_general | solution.py:52
  221.0 3.6 fusion.87
  224.6 4.3 fusion.88
  228.9 7.1 %fusion.91 = f32[1,1024,128]{2,1,0:T(8,128)S(1)} fusion(bf16[128,8,128]{0,2,1:T(8,128)(2,1)S(1)} %bitcast.121, f32[1024,128,8]{1,0,2:T(8,128)} %fusion.87, f32[8,128,1024]{1,2,0:T(8,128)} %get-tuple-element.238, f32[8,128]{1,0:T(8,128)S(1)} %get-tuple-element.239), kind=kOutput, calls=%fused_computation.19.clone.1 | convolution fusion | flops 275777536 | bytes 9179136 | tf_op jit(solution)/shard_map/while/body/eval_jaxpr/hqk,qhd->kd/dot_general | solution.py:55
  236.0 7.3 %fusion.89 = bf16[128,8,128]{2,0,1:T(8,128)(2,1)S(1)} fusion(f32[1024,128,8]{1,0,2:T(8,128)} %fusion.87, bf16[1,1024,1024]{2,1,0:T(8,128)(2,1)} %get-tuple-element.269, s32[]{:T(128)S(6)} %select_n.45, f32[8,128,1024]{1,2,0:T(8,128)} %get-tuple-element.238, f32[8,128]{1,0:T(8,128)S(1)} %get-tuple-element.239), kind=kOutput, calls=%fused_computation.21.clone.1 | convolution fusion | flops 275908608 | bytes 17309700 | tf_op jit(solution)/shard_map/while/body/eval_jaxpr/hqk,kd->qhd/dot_general | solution.py:52
  253.2 4.3 fusion.88
  257.4 7.1 %fusion.91 = f32[1,1024,128]{2,1,0:T(8,128)S(1)} fusion(bf16[128,8,128]{0,2,1:T(8,128)(2,1)S(1)} %bitcast.121, f32[1024,128,8]{1,0,2:T(8,128)} %fusion.87, f32[8,128,1024]{1,2,0:T(8,128)} %get-tuple-element.238, f32[8,128]{1,0:T(8,128)S(1)} %get-tuple-element.239), kind=kOutput, calls=%fused_computation.19.clone.1 | convolution fusion | flops 275777536 | bytes 9179136 | tf_op jit(solution)/shard_map/while/body/eval_jaxpr/hqk,qhd->kd/dot_general | solution.py:55
  264.5 7.3 %fusion.89 = bf16[128,8,128]{2,0,1:T(8,128)(2,1)S(1)} fusion(f32[1024,128,8]{1,0,2:T(8,128)} %fusion.87, bf16[1,1024,1024]{2,1,0:T(8,128)(2,1)} %get-tuple-element.269, s32[]{:T(128)S(6)} %select_n.45, f32[8,128,1024]{1,2,0:T(8,128)} %get-tuple-element.238, f32[8,128]{1,0:T(8,128)S(1)} %get-tuple-element.239), kind=kOutput, calls=%fused_computation.21.clone.1 | convolution fusion | flops 275908608 | bytes 17309700 | tf_op jit(solution)/shard_map/while/body/eval_jaxpr/hqk,kd->qhd/dot_general | solution.py:52
  281.7 4.3 fusion.88
  286.0 7.1 %fusion.91 = f32[1,1024,128]{2,1,0:T(8,128)S(1)} fusion(bf16[128,8,128]{0,2,1:T(8,128)(2,1)S(1)} %bitcast.121, f32[1024,128,8]{1,0,2:T(8,128)} %fusion.87, f32[8,128,1024]{1,2,0:T(8,128)} %get-tuple-element.238, f32[8,128]{1,0:T(8,128)S(1)} %get-tuple-element.239), kind=kOutput, calls=%fused_computation.19.clone.1 | convolution fusion | flops 275777536 | bytes 9179136 | tf_op jit(solution)/shard_map/while/body/eval_jaxpr/hqk,qhd->kd/dot_general | solution.py:55
  293.0 7.3 %fusion.89 = bf16[128,8,128]{2,0,1:T(8,128)(2,1)S(1)} fusion(f32[1024,128,8]{1,0,2:T(8,128)} %fusion.87, bf16[1,1024,1024]{2,1,0:T(8,128)(2,1)} %get-tuple-element.269, s32[]{:T(128)S(6)} %select_n.45, f32[8,128,1024]{1,2,0:T(8,128)} %get-tuple-element.238, f32[8,128]{1,0:T(8,128)S(1)} %get-tuple-element.239), kind=kOutput, calls=%fused_computation.21.clone.1 | convolution fusion | flops 275908608 | bytes 17309700 | tf_op jit(solution)/shard_map/while/body/eval_jaxpr/hqk,kd->qhd/dot_general | solution.py:52
  310.3 4.3 fusion.88
  314.5 7.1 %fusion.91 = f32[1,1024,128]{2,1,0:T(8,128)S(1)} fusion(bf16[128,8,128]{0,2,1:T(8,128)(2,1)S(1)} %bitcast.121, f32[1024,128,8]{1,0,2:T(8,128)} %fusion.87, f32[8,128,1024]{1,2,0:T(8,128)} %get-tuple-element.238, f32[8,128]{1,0:T(8,128)S(1)} %get-tuple-element.239), kind=kOutput, calls=%fused_computation.19.clone.1 | convolution fusion | flops 275777536 | bytes 9179136 | tf_op jit(solution)/shard_map/while/body/eval_jaxpr/hqk,qhd->kd/dot_general | solution.py:55
  321.6 7.3 %fusion.89 = bf16[128,8,128]{2,0,1:T(8,128)(2,1)S(1)} fusion(f32[1024,128,8]{1,0,2:T(8,128)} %fusion.87, bf16[1,1024,1024]{2,1,0:T(8,128)(2,1)} %get-tuple-element.269, s32[]{:T(128)S(6)} %select_n.45, f32[8,128,1024]{1,2,0:T(8,128)} %get-tuple-element.238, f32[8,128]{1,0:T(8,128)S(1)} %get-tuple-element.239), kind=kOutput, calls=%fused_computation.21.clone.1 | convolution fusion | flops 275908608 | bytes 17309700 | tf_op jit(solution)/shard_map/while/body/eval_jaxpr/hqk,kd->qhd/dot_general | solution.py:52
  337.7 90.9 %reduce-scatter.2.cloned.1.call-done = f32[2,128,1024]{2,1,0:T(8,128)} async-done(((f32[2,1024,1024]{2,1,0:T(8,128)}), f32[2,128,1024]{2,1,0:T(8,128)}) %reduce-scatter.2.cloned.1.call-update) | async-done | bytes 1048592 | tf_op jit(solution)/shard_map/reduce_scatter | solution.py:98
  429.9 17.4 %collective-permute-start.1 = (bf16[2,128,1024]{2,1,0:T(8,128)(2,1)S(1)}, bf16[2,128,1024]{2,1,0:T(8,128)(2,1)S(1)}, u32[]{:S(2)}, u32[]{:S(2)}) collective-permute-start(bf16[2,128,1024]{2,1,0:T(8,128)(2,1)S(1)} %convert_element_type.30), channel_id=1, source_target_pairs={{8,0},{16,8},{24,16},{32,24},{40,32},{48,40},{56,48},{64,56},{72,6... | collective-permute-start | bytes 1572872 | tf_op jit(solution)/shard_map/ppermute | solution.py:16
  447.3 6.7 %collective-permute-done.1 = bf16[2,128,1024]{2,1,0:T(8,128)(2,1)S(1)} collective-permute-done((bf16[2,128,1024]{2,1,0:T(8,128)(2,1)S(1)}, bf16[2,128,1024]{2,1,0:T(8,128)(2,1)S(1)}, u32[]{:S(2)}, u32[]{:S(2)}) %collective-permute-start.1) | collective-permute-done | bytes 524320 | tf_op jit(solution)/shard_map/ppermute | solution.py:16
  (82 shorter events, 90.6 us)
Async XLA Ops:
  7.2 47.2 %all-gather.3.cloned.1.call-start = ((), (), s32[]{:S(2)}) async-start(), calls=%async_computation.1 | async-start | bytes 2359296 | tf_op jit(solution)/shard_map/all_gather | solution.py:69
  7.9 91.6 %all-gather.5.cloned.1.call-start = ((), (), s32[]{:S(2)}) async-start(), calls=%async_computation.2 | async-start | bytes 2359296 | tf_op jit(solution)/shard_map/all_gather | solution.py:70
  8.6 420.0 %reduce-scatter.2.cloned.1.call-start = ((), (), s32[]{:S(2)}) async-start(), calls=%async_computation.3 | async-start | bytes 9437184 | tf_op jit(solution)/shard_map/reduce_scatter | solution.py:98
  333.7 1.6 copy-start
  335.3 112.0 %collective-permute-start = (bf16[1,128,8192]{2,1,0:T(8,128)(2,1)S(1)}, bf16[1,128,8192]{2,1,0:T(8,128)(2,1)}, u32[]{:S(2)}, u32[]{:S(2)}) collective-permute-start(bf16[1,128,8192]{2,1,0:T(8,128)(2,1)S(1)} %bitcast.123), channel_id=1, source_target_pairs={{8,0},{16,8},{24,16},{32,24},{40,32},{48,40},{56,48},{64,56},{72,6... | collective-permute-start | bytes 6291464 | tf_op jit(solution)/shard_map/ppermute | solution.py:16
  429.9 24.1 %collective-permute-start.1 = (bf16[2,128,1024]{2,1,0:T(8,128)(2,1)S(1)}, bf16[2,128,1024]{2,1,0:T(8,128)(2,1)S(1)}, u32[]{:S(2)}, u32[]{:S(2)}) collective-permute-start(bf16[2,128,1024]{2,1,0:T(8,128)(2,1)S(1)} %convert_element_type.30), channel_id=1, source_target_pairs={{8,0},{16,8},{24,16},{32,24},{40,32},{48,40},{56,48},{64,56},{72,6... | collective-permute-start | bytes 1572872 | tf_op jit(solution)/shard_map/ppermute | solution.py:16
Sparse Core Ops, SparseCore 0:
  9.8 44.5 all-gather.2
  56.2 43.3 all-gather.4
  333.9 94.7 reduce-scatter.1
where the time goes:
time: 466 us; the launch traced here: 464 us
  matrix products  201 us (43%)
  waiting for transfers between devices  187 us (40%)
  local copies, waits for them, and re-layouts  29.9 us (6%)
  starting transfers between devices  19.9 us (4%)
  between operations  13.8 us (3%)
  other arithmetic  12.6 us (3%)
    reduce_scatter x1, waiting for transfers between devices, per_device(): summed = lax.psum_scatter(pair_acc, 'ctx', scatter_dimension=1, tiled=True)  90.9 us
    dot_general x8, matrix products, head_block(): jnp.einsum('hqk,kd->qhd', score_grad, key_rows, preferred_element_type=jn...  58.1 us
    dot_general x8, matrix products, head_block(): jnp.einsum('hqk,qhd->kd', score_grad, query_heads, preferred_element_type...  56.6 us
    all_gather x1, waiting for transfers between devices, per_device(): lax.all_gather(value_states, 'ctx', axis=1, tiled=True)  45.2 us
    all_gather x1, waiting for transfers between devices, per_device(): lax.all_gather(key_states, 'ctx', axis=1, tiled=True)  42.9 us
    sub x8, matrix products, head_block(): exponent = jnp.exp(scores - row_max)  34 us
    dot_general x8, matrix products, head_block(): jnp.einsum('qhd,kd->hqk', grad_heads, value_rows, preferred_element_type=...  29 us
    dot_general x8, matrix products, head_block(): jnp.einsum('hqk,qhd->kd', attention_half, grad_heads, preferred_element_t...  23.1 us
  transfers between devices with their start and end apart: 5, of which 4 were waited for; matrix products, arithmetic and copies ran while one was open for 1% of the time, Pallas kernels for 0%

commit v1 on v0

--- a/solution.py
+++ b/solution.py
@@ -66,7 +66,9 @@
     allowed = allowed_mask(node_end[0], block_list[0], block_count[0])
     ratio = HEADS // KV_HEADS
     full_keys, full_values = (
-        lax.all_gather(key_states, "ctx", axis=1, tiled=True),
+        jnp.concatenate(
+            lax.all_to_all(jnp.stack([key_states] * lax.axis_size("ctx")), "ctx", 0, 0), axis=1
+        ),
         lax.all_gather(value_states, "ctx", axis=1, tiled=True),
     )
     length = full_keys.shape[1]

time: 466 us -> 438 us (0.940)
  waiting for transfers between devices: 187 us -> 146 us
  starting transfers between devices: 19.9 us -> 32.6 us
    all_gather x1 -> x0, waiting for transfers between devices: 42.9 us -> none  [per_device(): lax.all_gather(key_states, 'ctx', axis=1, tiled=True)]
    all_to_all x0 -> x1, waiting for transfers between devices: none -> 36.1 us  [per_device(): lax.all_to_all(jnp.stack([key_states] * lax.axis_size('ctx')), 'ctx', 0, 0)]
    all_gather x1, waiting for transfers between devices: 45.2 us -> 11.8 us  [per_device(): lax.all_gather(value_states, 'ctx', axis=1, tiled=True)]
    all_to_all x0 -> x1, starting transfers between devices: none -> 6.45 us  [per_device(): lax.all_to_all(jnp.stack([key_states] * lax.axis_size('ctx')), 'ctx', 0, 0)]
    ppermute x2, starting transfers between devices: 19.8 us -> 26.2 us  [from_behind(): return lax.ppermute(block, axis, route)]
where the time goes in v1:
time: 438 us; the launch traced here: 437 us
  matrix products  201 us (46%)
  waiting for transfers between devices  146 us (33%)
  starting transfers between devices  32.6 us (7%)
  local copies, waits for them, and re-layouts  32.4 us (7%)
  between operations  14.1 us (3%)
  other arithmetic  10.6 us (2%)
    reduce_scatter x1, waiting for transfers between devices, per_device(): summed = lax.psum_scatter(pair_acc, 'ctx', scatter_dimension=1, tiled=True)  90.6 us
    dot_general x8, matrix products, head_block(): jnp.einsum('hqk,kd->qhd', score_grad, key_rows, preferred_element_type=jn...  58.1 us
    dot_general x8, matrix products, head_block(): jnp.einsum('hqk,qhd->kd', score_grad, query_heads, preferred_element_type...  56.6 us
    all_to_all x1, waiting for transfers between devices, per_device(): lax.all_to_all(jnp.stack([key_states] * lax.axis_size('ctx')), 'ctx', 0, 0)  36.1 us
    sub x8, matrix products, head_block(): exponent = jnp.exp(scores - row_max)  34 us
    dot_general x8, matrix products, head_block(): jnp.einsum('qhd,kd->hqk', grad_heads, value_rows, preferred_element_type=...  29 us
    ppermute x2, starting transfers between devices, from_behind(): return lax.ppermute(block, axis, route)  26.2 us
    dot_general x8, matrix products, head_block(): jnp.einsum('hqk,qhd->kd', attention_half, grad_heads, preferred_element_t...  23.1 us
  transfers between devices with their start and end apart: 5, of which 4 were waited for; matrix products, arithmetic and copies ran while one was open for 1% of the time, Pallas kernels for 0%

profile of v1, /device:TPU:6, one launch (start us, length us, event | category | flops | bytes accessed | tf_op | source)
XLA Modules:
  0.0 436.8 jit_solution(13315281609352339937)
XLA Ops:
  10.5 6.5 %all-to-all-start = ((bf16[8,1,128,1024]{3,2,1,0:T(8,128)(2,1)}), bf16[8,1,128,1024]{3,2,1,0:T(8,128)(2,1)}, u32[]{:S(2)}, u32[]{:S(2)}) async-start(bf16[8,1,128,1024]{3,2,1,0:T(8,128)(2,1)} %stack.32), calls=%async_computation | async-start | bytes 4194304 | tf_op jit(solution)/shard_map/all_to_all | solution.py:70
  17.7 36.1 %all-to-all-done = bf16[8,1,128,1024]{3,2,1,0:T(8,128)(2,1)} async-done(((bf16[8,1,128,1024]{3,2,1,0:T(8,128)(2,1)}), bf16[8,1,128,1024]{3,2,1,0:T(8,128)(2,1)}, u32[]{:S(2)}, u32[]{:S(2)}) %all-to-all-start) | async-done | bytes 2097184 | tf_op jit(solution)/shard_map/all_to_all | solution.py:70
  53.8 11.8 %all-gather.2.cloned.1.call-done = bf16[1,1024,1024]{2,1,0:T(8,128)(2,1)} async-done(((bf16[1,128,1024]{2,1,0:T(8,128)(2,1)}), bf16[1,1024,1024]{2,1,0:T(8,128)(2,1)}) %all-gather.2.cloned.1.call-update) | async-done | bytes 2097168 | tf_op jit(solution)/shard_map/all_gather | solution.py:72
  67.1 4.3 broadcast_in_dim.57
  71.4 228.3 %while.15 = (s32[]{:T(128)}, bf16[128,8192]{1,0:T(8,128)(2,1)}, f32[2,1024,1024]{2,1,0:T(8,128)}, bf16[8,1,128,1024]{3,2,0,1:T(8,128)(2,1)}, pred[128,1024]{0,1:...) while((s32[]{:T(128)}, bf16[128,8192]{1,0:T(8,128)(2,1)}, ...), condition=%wide.region_5.6_spmd, body=%wide.region_1.5_spmd.sunk | while | flops 1363547136 | bytes 46289144 | solution.py:99
  76.5 4.2 fusion.88
  80.7 7.1 %fusion.91 = f32[1,1024,128]{2,1,0:T(8,128)S(1)} fusion(bf16[128,8,128]{0,2,1:T(8,128)(2,1)S(1)} %bitcast.124, f32[1024,128,8]{1,0,2:T(8,128)} %fusion.87, f32[8,128,1024]{1,2,0:T(8,128)} %get-tuple-element.246, f32[8,128]{1,0:T(8,128)S(1)} %get-tuple-element.247), kind=kOutput, calls=%fused_computation.19.clone.1 | convolution fusion | flops 275777536 | bytes 9179136 | tf_op jit(solution)/shard_map/while/body/eval_jaxpr/hqk,qhd->kd/dot_general | solution.py:55
  87.8 7.3 %fusion.89 = bf16[128,8,128]{2,0,1:T(8,128)(2,1)S(1)} fusion(f32[1024,128,8]{1,0,2:T(8,128)} %fusion.87, bf16[1024,1024]{1,0:T(8,128)(2,1)} %bitcast.118, s32[]{:T(128)S(6)} %select_n.45, f32[8,128,1024]{1,2,0:T(8,128)} %get-tuple-element.246, f32[8,128]{1,0:T(8,128)S(1)} %get-tuple-element.247), kind=kOutput, calls=%fused_computation.21.clone.1 | convolution fusion | flops 275908608 | bytes 17309700 | tf_op jit(solution)/shard_map/while/body/eval_jaxpr/hqk,kd->qhd/dot_general | solution.py:52
  105.0 4.2 fusion.88
  109.2 7.1 %fusion.91 = f32[1,1024,128]{2,1,0:T(8,128)S(1)} fusion(bf16[128,8,128]{0,2,1:T(8,128)(2,1)S(1)} %bitcast.124, f32[1024,128,8]{1,0,2:T(8,128)} %fusion.87, f32[8,128,1024]{1,2,0:T(8,128)} %get-tuple-element.246, f32[8,128]{1,0:T(8,128)S(1)} %get-tuple-element.247), kind=kOutput, calls=%fused_computation.19.clone.1 | convolution fusion | flops 275777536 | bytes 9179136 | tf_op jit(solution)/shard_map/while/body/eval_jaxpr/hqk,qhd->kd/dot_general | solution.py:55
  116.3 7.3 %fusion.89 = bf16[128,8,128]{2,0,1:T(8,128)(2,1)S(1)} fusion(f32[1024,128,8]{1,0,2:T(8,128)} %fusion.87, bf16[1024,1024]{1,0:T(8,128)(2,1)} %bitcast.118, s32[]{:T(128)S(6)} %select_n.45, f32[8,128,1024]{1,2,0:T(8,128)} %get-tuple-element.246, f32[8,128]{1,0:T(8,128)S(1)} %get-tuple-element.247), kind=kOutput, calls=%fused_computation.21.clone.1 | convolution fusion | flops 275908608 | bytes 17309700 | tf_op jit(solution)/shard_map/while/body/eval_jaxpr/hqk,kd->qhd/dot_general | solution.py:52
  133.5 4.2 fusion.88
  137.8 7.1 %fusion.91 = f32[1,1024,128]{2,1,0:T(8,128)S(1)} fusion(bf16[128,8,128]{0,2,1:T(8,128)(2,1)S(1)} %bitcast.124, f32[1024,128,8]{1,0,2:T(8,128)} %fusion.87, f32[8,128,1024]{1,2,0:T(8,128)} %get-tuple-element.246, f32[8,128]{1,0:T(8,128)S(1)} %get-tuple-element.247), kind=kOutput, calls=%fused_computation.19.clone.1 | convolution fusion | flops 275777536 | bytes 9179136 | tf_op jit(solution)/shard_map/while/body/eval_jaxpr/hqk,qhd->kd/dot_general | solution.py:55
  144.8 7.3 %fusion.89 = bf16[128,8,128]{2,0,1:T(8,128)(2,1)S(1)} fusion(f32[1024,128,8]{1,0,2:T(8,128)} %fusion.87, bf16[1024,1024]{1,0:T(8,128)(2,1)} %bitcast.118, s32[]{:T(128)S(6)} %select_n.45, f32[8,128,1024]{1,2,0:T(8,128)} %get-tuple-element.246, f32[8,128]{1,0:T(8,128)S(1)} %get-tuple-element.247), kind=kOutput, calls=%fused_computation.21.clone.1 | convolution fusion | flops 275908608 | bytes 17309700 | tf_op jit(solution)/shard_map/while/body/eval_jaxpr/hqk,kd->qhd/dot_general | solution.py:52
  166.3 7.1 %fusion.91 = f32[1,1024,128]{2,1,0:T(8,128)S(1)} fusion(bf16[128,8,128]{0,2,1:T(8,128)(2,1)S(1)} %bitcast.124, f32[1024,128,8]{1,0,2:T(8,128)} %fusion.87, f32[8,128,1024]{1,2,0:T(8,128)} %get-tuple-element.246, f32[8,128]{1,0:T(8,128)S(1)} %get-tuple-element.247), kind=kOutput, calls=%fused_computation.19.clone.1 | convolution fusion | flops 275777536 | bytes 9179136 | tf_op jit(solution)/shard_map/while/body/eval_jaxpr/hqk,qhd->kd/dot_general | solution.py:55
  173.4 7.3 %fusion.89 = bf16[128,8,128]{2,0,1:T(8,128)(2,1)S(1)} fusion(f32[1024,128,8]{1,0,2:T(8,128)} %fusion.87, bf16[1024,1024]{1,0:T(8,128)(2,1)} %bitcast.118, s32[]{:T(128)S(6)} %select_n.45, f32[8,128,1024]{1,2,0:T(8,128)} %get-tuple-element.246, f32[8,128]{1,0:T(8,128)S(1)} %get-tuple-element.247), kind=kOutput, calls=%fused_computation.21.clone.1 | convolution fusion | flops 275908608 | bytes 17309700 | tf_op jit(solution)/shard_map/while/body/eval_jaxpr/hqk,kd->qhd/dot_general | solution.py:52
  190.6 4.2 fusion.88
  194.8 7.1 %fusion.91 = f32[1,1024,128]{2,1,0:T(8,128)S(1)} fusion(bf16[128,8,128]{0,2,1:T(8,128)(2,1)S(1)} %bitcast.124, f32[1024,128,8]{1,0,2:T(8,128)} %fusion.87, f32[8,128,1024]{1,2,0:T(8,128)} %get-tuple-element.246, f32[8,128]{1,0:T(8,128)S(1)} %get-tuple-element.247), kind=kOutput, calls=%fused_computation.19.clone.1 | convolution fusion | flops 275777536 | bytes 9179136 | tf_op jit(solution)/shard_map/while/body/eval_jaxpr/hqk,qhd->kd/dot_general | solution.py:55
  201.9 7.3 %fusion.89 = bf16[128,8,128]{2,0,1:T(8,128)(2,1)S(1)} fusion(f32[1024,128,8]{1,0,2:T(8,128)} %fusion.87, bf16[1024,1024]{1,0:T(8,128)(2,1)} %bitcast.118, s32[]{:T(128)S(6)} %select_n.45, f32[8,128,1024]{1,2,0:T(8,128)} %get-tuple-element.246, f32[8,128]{1,0:T(8,128)S(1)} %get-tuple-element.247), kind=kOutput, calls=%fused_computation.21.clone.1 | convolution fusion | flops 275908608 | bytes 17309700 | tf_op jit(solution)/shard_map/while/body/eval_jaxpr/hqk,kd->qhd/dot_general | solution.py:52
  219.2 4.2 fusion.88
  223.4 7.1 %fusion.91 = f32[1,1024,128]{2,1,0:T(8,128)S(1)} fusion(bf16[128,8,128]{0,2,1:T(8,128)(2,1)S(1)} %bitcast.124, f32[1024,128,8]{1,0,2:T(8,128)} %fusion.87, f32[8,128,1024]{1,2,0:T(8,128)} %get-tuple-element.246, f32[8,128]{1,0:T(8,128)S(1)} %get-tuple-element.247), kind=kOutput, calls=%fused_computation.19.clone.1 | convolution fusion | flops 275777536 | bytes 9179136 | tf_op jit(solution)/shard_map/while/body/eval_jaxpr/hqk,qhd->kd/dot_general | solution.py:55
  230.5 7.3 %fusion.89 = bf16[128,8,128]{2,0,1:T(8,128)(2,1)S(1)} fusion(f32[1024,128,8]{1,0,2:T(8,128)} %fusion.87, bf16[1024,1024]{1,0:T(8,128)(2,1)} %bitcast.118, s32[]{:T(128)S(6)} %select_n.45, f32[8,128,1024]{1,2,0:T(8,128)} %get-tuple-element.246, f32[8,128]{1,0:T(8,128)S(1)} %get-tuple-element.247), kind=kOutput, calls=%fused_computation.21.clone.1 | convolution fusion | flops 275908608 | bytes 17309700 | tf_op jit(solution)/shard_map/while/body/eval_jaxpr/hqk,kd->qhd/dot_general | solution.py:52
  247.7 4.2 fusion.88
  252.0 7.1 %fusion.91 = f32[1,1024,128]{2,1,0:T(8,128)S(1)} fusion(bf16[128,8,128]{0,2,1:T(8,128)(2,1)S(1)} %bitcast.124, f32[1024,128,8]{1,0,2:T(8,128)} %fusion.87, f32[8,128,1024]{1,2,0:T(8,128)} %get-tuple-element.246, f32[8,128]{1,0:T(8,128)S(1)} %get-tuple-element.247), kind=kOutput, calls=%fused_computation.19.clone.1 | convolution fusion | flops 275777536 | bytes 9179136 | tf_op jit(solution)/shard_map/while/body/eval_jaxpr/hqk,qhd->kd/dot_general | solution.py:55
  259.0 7.3 %fusion.89 = bf16[128,8,128]{2,0,1:T(8,128)(2,1)S(1)} fusion(f32[1024,128,8]{1,0,2:T(8,128)} %fusion.87, bf16[1024,1024]{1,0:T(8,128)(2,1)} %bitcast.118, s32[]{:T(128)S(6)} %select_n.45, f32[8,128,1024]{1,2,0:T(8,128)} %get-tuple-element.246, f32[8,128]{1,0:T(8,128)S(1)} %get-tuple-element.247), kind=kOutput, calls=%fused_computation.21.clone.1 | convolution fusion | flops 275908608 | bytes 17309700 | tf_op jit(solution)/shard_map/while/body/eval_jaxpr/hqk,kd->qhd/dot_general | solution.py:52
  276.2 4.2 fusion.88
  280.5 7.1 %fusion.91 = f32[1,1024,128]{2,1,0:T(8,128)S(1)} fusion(bf16[128,8,128]{0,2,1:T(8,128)(2,1)S(1)} %bitcast.124, f32[1024,128,8]{1,0,2:T(8,128)} %fusion.87, f32[8,128,1024]{1,2,0:T(8,128)} %get-tuple-element.246, f32[8,128]{1,0:T(8,128)S(1)} %get-tuple-element.247), kind=kOutput, calls=%fused_computation.19.clone.1 | convolution fusion | flops 275777536 | bytes 9179136 | tf_op jit(solution)/shard_map/while/body/eval_jaxpr/hqk,qhd->kd/dot_general | solution.py:55
  287.6 7.3 %fusion.89 = bf16[128,8,128]{2,0,1:T(8,128)(2,1)S(1)} fusion(f32[1024,128,8]{1,0,2:T(8,128)} %fusion.87, bf16[1024,1024]{1,0:T(8,128)(2,1)} %bitcast.118, s32[]{:T(128)S(6)} %select_n.45, f32[8,128,1024]{1,2,0:T(8,128)} %get-tuple-element.246, f32[8,128]{1,0:T(8,128)S(1)} %get-tuple-element.247), kind=kOutput, calls=%fused_computation.21.clone.1 | convolution fusion | flops 275908608 | bytes 17309700 | tf_op jit(solution)/shard_map/while/body/eval_jaxpr/hqk,kd->qhd/dot_general | solution.py:52
  301.3 8.0 %collective-permute-start = (bf16[1,128,8192]{2,1,0:T(8,128)(2,1)S(1)}, bf16[1,128,8192]{2,1,0:T(8,128)(2,1)}, u32[]{:S(2)}, u32[]{:S(2)}) collective-permute-start(bf16[1,128,8192]{2,1,0:T(8,128)(2,1)S(1)} %bitcast.126), channel_id=1, source_target_pairs={{8,0},{16,8},{24,16},{32,24},{40,32},{48,40},{56,48},{64,56},{72,6... | collective-permute-start | bytes 6291464 | tf_op jit(solution)/shard_map/ppermute | solution.py:16
  309.3 90.6 %reduce-scatter.2.cloned.1.call-done = f32[2,128,1024]{2,1,0:T(8,128)} async-done(((f32[2,1024,1024]{2,1,0:T(8,128)}), f32[2,128,1024]{2,1,0:T(8,128)}) %reduce-scatter.2.cloned.1.call-update) | async-done | bytes 1048592 | tf_op jit(solution)/shard_map/reduce_scatter | solution.py:100
  401.2 18.1 %collective-permute-start.1 = (bf16[2,128,1024]{2,1,0:T(8,128)(2,1)S(1)}, bf16[2,128,1024]{2,1,0:T(8,128)(2,1)S(1)}, u32[]{:S(2)}, u32[]{:S(2)}) collective-permute-start(bf16[2,128,1024]{2,1,0:T(8,128)(2,1)S(1)} %convert_element_type.30), channel_id=1, source_target_pairs={{8,0},{16,8},{24,16},{32,24},{40,32},{48,40},{56,48},{64,56},{72,6... | collective-permute-start | bytes 1572872 | tf_op jit(solution)/shard_map/ppermute | solution.py:16
  419.4 6.7 %collective-permute-done.1 = bf16[2,128,1024]{2,1,0:T(8,128)(2,1)S(1)} collective-permute-done((bf16[2,128,1024]{2,1,0:T(8,128)(2,1)S(1)}, bf16[2,128,1024]{2,1,0:T(8,128)(2,1)S(1)}, u32[]{:S(2)}, u32[]{:S(2)}) %collective-permute-start.1) | collective-permute-done | bytes 524320 | tf_op jit(solution)/shard_map/ppermute | solution.py:16
  (88 shorter events, 95.9 us)
Async XLA Ops:
  7.2 9.8 %copy-start.3 = (s32[1,8]{1,0:T(1,128)S(1)}, s32[1,8]{1,0:T(1,128)}, u32[]{:S(2)}) copy-start(s32[1,8]{1,0:T(1,128)} %param.15) | copy-start | bytes 100
  7.2 9.8 %copy-start.2 = (s32[1,8,8]{2,1,0:T(8,128)S(1)}, s32[1,8,8]{2,1,0:T(8,128)}, u32[]{:S(2)}) copy-start(s32[1,8,8]{2,1,0:T(8,128)} %param.14) | copy-start | bytes 772
  7.2 10.3 %copy-start.1 = (s32[1,1024]{1,0:T(1,128)S(1)}, s32[1,1024]{1,0:T(1,128)}, u32[]{:S(2)}) copy-start(s32[1,1024]{1,0:T(1,128)} %param.13) | copy-start | bytes 12292
  7.2 58.4 %all-gather.2.cloned.1.call-start = ((), (), s32[]{:S(2)}) async-start(), calls=%async_computation.2 | async-start | bytes 2359296 | tf_op jit(solution)/shard_map/all_gather | solution.py:72
  10.5 43.3 %all-to-all-start = ((bf16[8,1,128,1024]{3,2,1,0:T(8,128)(2,1)}), bf16[8,1,128,1024]{3,2,1,0:T(8,128)(2,1)}, u32[]{:S(2)}, u32[]{:S(2)}) async-start(bf16[8,1,128,1024]{3,2,1,0:T(8,128)(2,1)} %stack.32), calls=%async_computation | async-start | bytes 4194304 | tf_op jit(solution)/shard_map/all_to_all | solution.py:70
  16.9 383.0 %reduce-scatter.2.cloned.1.call-start = ((), (), s32[]{:S(2)}) async-start(), calls=%async_computation.3 | async-start | bytes 9437184 | tf_op jit(solution)/shard_map/reduce_scatter | solution.py:100
  299.7 1.6 copy-start
  301.3 118.0 %collective-permute-start = (bf16[1,128,8192]{2,1,0:T(8,128)(2,1)S(1)}, bf16[1,128,8192]{2,1,0:T(8,128)(2,1)}, u32[]{:S(2)}, u32[]{:S(2)}) collective-permute-start(bf16[1,128,8192]{2,1,0:T(8,128)(2,1)S(1)} %bitcast.126), channel_id=1, source_target_pairs={{8,0},{16,8},{24,16},{32,24},{40,32},{48,40},{56,48},{64,56},{72,6... | collective-permute-start | bytes 6291464 | tf_op jit(solution)/shard_map/ppermute | solution.py:16
  401.2 24.8 %collective-permute-start.1 = (bf16[2,128,1024]{2,1,0:T(8,128)(2,1)S(1)}, bf16[2,128,1024]{2,1,0:T(8,128)(2,1)S(1)}, u32[]{:S(2)}, u32[]{:S(2)}) collective-permute-start(bf16[2,128,1024]{2,1,0:T(8,128)(2,1)S(1)} %convert_element_type.30), channel_id=1, source_target_pairs={{8,0},{16,8},{24,16},{32,24},{40,32},{48,40},{56,48},{64,56},{72,6... | collective-permute-start | bytes 1572872 | tf_op jit(solution)/shard_map/ppermute | solution.py:16
Sparse Core Ops, SparseCore 0:
  9.8 55.7 all-gather.1
  299.9 99.9 reduce-scatter.1
